TPU v7x, 512 devices: a whole 4x8x8 slice. The times are simulated.
512 devices in a mesh: seq: 64 (over x, z_lo, y), chan: 8 (over z_hi, core).
Axes of the slice: x: 4, y: 8, z: 8 (z_hi: 4, z_lo: 2; z = z_hi * 2 + z_lo), core: 2. Of those that a mesh axis runs over, the one named last changes fastest.
Arguments:
- token_ids: int32 [8192], P('seq'), may hold values from 0 to 511
- vocab_table: bfloat16 [512, 4, 4096], P(None, None, 'chan'), may hold values from -6 to 6
- short_taps: bfloat16 [3, 3, 4096], P(None, None, 'chan'), may hold values from -3 to 3
- filter_spec: bfloat16 [2, 128, 128, 4096], P(None, 'seq', None, 'chan'), may hold values from -6 to 6
- out_weight: bfloat16 [4096, 4096], P('chan', 'seq'), may hold values from -0.25 to 0.25
Outputs:
- mixed: bfloat16 [8192, 4096], P('seq', 'chan')
- gated: bfloat16 [8192, 4096], P('seq', 'chan')
All inputs are finite; a program needn't handle non-finite values.
Results may differ from a plain program's by a relative error of at most 0.02.
Values may be sent and summed in bfloat16 or wider, within the bound.
A program may use at most 64 MiB of HBM per device.

v0:
```python
import math

import jax
import jax.numpy as jnp
from jax import lax
from jax.sharding import PartitionSpec as P


def from_behind(block, axis, distance):
    devices = range(lax.axis_size(axis))
    route = [(i - distance, i) for i in devices if i - distance in devices]
    return lax.ppermute(block, axis, route)


def contract(pattern, operand, table):
    return jnp.einsum(
        pattern, operand, table, precision=lax.Precision.HIGHEST, preferred_element_type=jnp.float32
    )


def angle_table(row_count, col_count, modulus, row_start):
    row_ids = row_start + jnp.arange(row_count, dtype=jnp.int32)
    col_ids = jnp.arange(col_count, dtype=jnp.int32)
    product = row_ids[:, None] * col_ids[None, :] % modulus
    angles = product.astype(jnp.float32) * (2.0 * math.pi / modulus)
    return (jnp.cos(angles), jnp.sin(angles))


def rotate_real(real_part, cos_table, sin_table, pattern, direction):
    return (
        contract(pattern, real_part, cos_table),
        direction * contract(pattern, real_part, sin_table),
    )


def rotate(real_part, imag_part, cos_table, sin_table, pattern, direction):
    real_cos = contract(pattern, real_part, cos_table)
    real_sin = contract(pattern, real_part, sin_table)
    imag_cos = contract(pattern, imag_part, cos_table)
    imag_sin = contract(pattern, imag_part, sin_table)
    return (real_cos - direction * imag_sin, imag_cos + direction * real_sin)


def twist(real_part, imag_part, cos_table, sin_table, direction):
    return (
        real_part * cos_table - direction * imag_part * sin_table,
        imag_part * cos_table + direction * real_part * sin_table,
    )


def times_spectrum(real_part, imag_part, spec_real, spec_imag):
    return (
        real_part * spec_real - imag_part * spec_imag,
        real_part * spec_imag + imag_part * spec_real,
    )


def per_device(token_ids, vocab_table, short_taps, filter_spec, out_weight):
    tok_rows = token_ids.shape[0]
    vocab_size = vocab_table.shape[0]
    channels = vocab_table.shape[2]
    one_hot = (token_ids[:, None] == jnp.arange(vocab_size, dtype=jnp.int32)[None, :]).astype(
        jnp.bfloat16
    )
    features = jnp.dot(
        one_hot, vocab_table.reshape(vocab_size, 4 * channels), preferred_element_type=jnp.float32
    )
    features = features.astype(jnp.bfloat16).reshape(tok_rows, 4, channels)
    earlier = from_behind(features[tok_rows - 2 :, :3, :], "seq", 1)
    extended = jnp.concatenate([earlier, features[:, :3, :]], 0).astype(jnp.float32)
    weights = short_taps.astype(jnp.float32)
    shortened = (
        weights[:, 0] * extended[2:]
        + weights[:, 1] * extended[1:-1]
        + weights[:, 2] * extended[:-2]
    )
    signal = (shortened[:, 1] * shortened[:, 2]).astype(jnp.bfloat16)
    devices = lax.axis_size("seq")
    position = lax.axis_index("seq")
    padded_length = 2 * devices * tok_rows
    inverse_length = 1.0 / padded_length
    block_cos, block_sin = angle_table(devices, 2 * devices, 2 * devices, 0)
    row_cos, row_sin = angle_table(tok_rows, tok_rows, tok_rows, 0)
    slab_rows = tok_rows // devices
    pieces = signal.reshape(1, devices, slab_rows, channels)
    received = lax.all_to_all(pieces, "seq", split_axis=1, concat_axis=0, tiled=True)
    received = received.reshape(devices, slab_rows, channels).astype(jnp.float32)
    first_re, first_im = rotate_real(received, block_cos, block_sin, "prc,pa->arc", -1.0)
    twid_cos, twid_sin = angle_table(slab_rows, 2 * devices, padded_length, position * slab_rows)
    twid_cos = twid_cos.T[:, :, None]
    twid_sin = twid_sin.T[:, :, None]
    first_re, first_im = twist(first_re, first_im, twid_cos, twid_sin, -1.0)
    sent = (
        first_re.reshape(2 * devices, 1, slab_rows, channels),
        first_im.reshape(2 * devices, 1, slab_rows, channels),
    )
    owned_re, owned_im = (
        lax.all_to_all(
            sent[0].astype(jnp.bfloat16), "seq", split_axis=0, concat_axis=1, tiled=True
        ).astype(jnp.float32),
        lax.all_to_all(
            sent[1].astype(jnp.bfloat16), "seq", split_axis=0, concat_axis=1, tiled=True
        ).astype(jnp.float32),
    )
    owned_re = owned_re.reshape(2, tok_rows, channels)
    owned_im = owned_im.reshape(2, tok_rows, channels)
    freq_re, freq_im = rotate(owned_re, owned_im, row_cos, row_sin, "amc,mb->abc", -1.0)
    freq_re, freq_im = times_spectrum(
        freq_re, freq_im, filter_spec[0].astype(jnp.float32), filter_spec[1].astype(jnp.float32)
    )
    back_re, back_im = rotate(freq_re, freq_im, row_cos, row_sin, "abc,bm->amc", 1.0)
    returned = (
        back_re.reshape(2, devices, slab_rows, channels),
        back_im.reshape(2, devices, slab_rows, channels),
    )
    local_re, local_im = (
        lax.all_to_all(
            returned[0].astype(jnp.bfloat16), "seq", split_axis=1, concat_axis=0, tiled=True
        ).astype(jnp.float32),
        lax.all_to_all(
            returned[1].astype(jnp.bfloat16), "seq", split_axis=1, concat_axis=0, tiled=True
        ).astype(jnp.float32),
    )
    local_re = local_re.reshape(2 * devices, slab_rows, channels)
    local_im = local_im.reshape(2 * devices, slab_rows, channels)
    local_re, local_im = twist(local_re, local_im, twid_cos, twid_sin, 1.0)
    result = (
        contract("arc,pa->prc", local_re, block_cos) - contract("arc,pa->prc", local_im, block_sin)
    ) * inverse_length
    arrived = lax.all_to_all(
        result.reshape(devices, 1, slab_rows, channels).astype(jnp.bfloat16),
        "seq",
        split_axis=0,
        concat_axis=1,
        tiled=True,
    ).astype(jnp.float32)
    conv = arrived.reshape(tok_rows, channels)
    gated = (shortened[:, 0] * conv).astype(jnp.bfloat16)
    partial_value = jnp.dot(
        gated,
        lax.all_gather(out_weight, "seq", axis=1, tiled=True),
        preferred_element_type=jnp.float32,
    )
    summed = lax.psum_scatter(
        partial_value.astype(jnp.bfloat16), "chan", scatter_dimension=1, tiled=True
    ).astype(jnp.float32)
    mixed = (features[:, 3, :].astype(jnp.float32) + summed).astype(jnp.bfloat16)
    return (mixed, gated)


def solution(mesh):
    placed = (
        P("seq"),
        P(None, None, "chan"),
        P(None, None, "chan"),
        P(None, "seq", None, "chan"),
        P("chan", "seq"),
    )
    return jax.shard_map(
        per_device,
        mesh=mesh,
        in_specs=placed,
        out_specs=(P("seq", "chan"), P("seq", "chan")),
        check_vma=False,
    )
```

profile of v0, /device:TPU:1, one launch (start us, length us, event | category | flops | bytes accessed | tf_op | source)
XLA Modules:
  0.0 374.2 jit_solution(8718628768705930076)
XLA Ops:
  7.2 0.0 all-gather.2.cloned.1.call-start
  7.2 0.7 all-gather.2.cloned.1.call-update
  7.9 0.0 copy-start.3
  7.9 2.2 copy.45
  10.1 0.0 copy-start.2
  10.1 0.0 copy-done.3
  10.2 0.5 convolution_convert_fusion.1
  10.6 0.4 reshape.150
  11.0 4.0 %collective-permute-start = (bf16[2,3,512]{2,0,1:T(2,128)(2,1)S(1)}, bf16[2,3,512]{2,0,1:T(2,128)(2,1)S(1)}, u32[]{:S(2)}, u32[]{:S(2)}) collective-permute-start(bf16[2,3,512]{2,0,1:T(2,128)(2,1)S(1)} %copy.43), channel_id=1, source_target_pairs={{0,8},{8,16},{16,24},{24,32},{32,40},{40,48},{48,56},{56,64},{64,7... | collective-permute-start | bytes 18440 | tf_op jit(solution)/shard_map/ppermute | solution.py:12
  15.1 0.0 copy-done.2
  15.1 0.1 copy.44
  15.2 0.6 collective-permute-done
  15.8 0.1 maximum_convert_fusion
  16.0 0.2 fusion.11
  16.3 0.7 convert_element_type.177
  17.0 13.7 %all-to-all-start = ((bf16[1,64,2,512]{3,2,0,1:T(2,128)(2,1)}), bf16[1,64,2,512]{3,2,0,1:T(2,128)(2,1)S(1)}, u32[]{:S(2)}, u32[]{:S(2)}) async-start(bf16[1,64,2,512]{3,2,0,1:T(2,128)(2,1)} %bitcast.4), calls=%async_computation | async-start | bytes 262144 | tf_op jit(solution)/shard_map/all_to_all | solution.py:86
  30.7 0.1 broadcast_multiply_fusion.1
  30.8 10.4 %all-to-all-done = bf16[1,64,2,512]{3,2,0,1:T(2,128)(2,1)S(1)} async-done(((bf16[1,64,2,512]{3,2,0,1:T(2,128)(2,1)}), bf16[1,64,2,512]{3,2,0,1:T(2,128)(2,1)S(1)}, u32[]{:S(2)}, u32[]{:S(2)}) %all-to-all-start) | async-done | bytes 131104 | tf_op jit(solution)/shard_map/all_to_all | solution.py:86
  41.2 0.5 fusion.32
  41.7 0.6 fusion.23
  42.4 1.0 copy.30
  43.4 4.6 %all-to-all-start.2 = ((bf16[128,1,2,512]{3,2,1,0:T(2,128)(2,1)}), bf16[128,1,2,512]{3,2,1,0:T(2,128)(2,1)S(1)}, u32[]{:S(2)}, u32[]{:S(2)}) async-start(bf16[128,1,2,512]{3,2,1,0:T(2,128)(2,1)} %copy.30), calls=%async_computation.2 | async-start | bytes 524288 | tf_op jit(solution)/shard_map/all_to_all | solution.py:101
  48.0 1.0 copy.28
  49.0 10.4 %all-to-all-done.2 = bf16[128,1,2,512]{3,2,1,0:T(2,128)(2,1)S(1)} async-done(((bf16[128,1,2,512]{3,2,1,0:T(2,128)(2,1)}), bf16[128,1,2,512]{3,2,1,0:T(2,128)(2,1)S(1)}, u32[]{:S(2)}, u32[]{:S(2)}) %all-to-all-start.2) | async-done | bytes 262176 | tf_op jit(solution)/shard_map/all_to_all | solution.py:101
  59.4 4.9 %all-to-all-start.1 = ((bf16[128,1,2,512]{3,2,1,0:T(2,128)(2,1)}), bf16[128,1,2,512]{3,2,1,0:T(2,128)(2,1)S(1)}, u32[]{:S(2)}, u32[]{:S(2)}) async-start(bf16[128,1,2,512]{3,2,1,0:T(2,128)(2,1)} %copy.28), calls=%async_computation.1 | async-start | bytes 524288 | tf_op jit(solution)/shard_map/all_to_all | solution.py:98
  64.4 0.2 copy.64
  64.6 0.1 reshape.153
  64.7 11.3 %all-to-all-done.1 = bf16[128,1,2,512]{3,2,1,0:T(2,128)(2,1)S(1)} async-done(((bf16[128,1,2,512]{3,2,1,0:T(2,128)(2,1)}), bf16[128,1,2,512]{3,2,1,0:T(2,128)(2,1)S(1)}, u32[]{:S(2)}, u32[]{:S(2)}) %all-to-all-start.1) | async-done | bytes 262176 | tf_op jit(solution)/shard_map/all_to_all | solution.py:98
  76.0 0.2 copy.65
  76.2 0.1 reshape.152
  76.3 0.0 copy-start
  76.3 0.6 fusion.50
  76.9 0.6 fusion.52
  77.5 0.6 fusion.1
  78.1 0.6 fusion.3
  78.7 0.0 copy-done
  78.7 0.9 fusion.48
  79.7 0.9 fusion.7
  80.6 1.0 copy.37
  81.6 4.9 %all-to-all-start.3 = ((bf16[2,64,2,512]{3,0,2,1:T(2,128)(2,1)}), bf16[2,64,2,512]{3,0,2,1:T(2,128)(2,1)S(1)}, u32[]{:S(2)}, u32[]{:S(2)}) async-start(bf16[2,64,2,512]{3,0,2,1:T(2,128)(2,1)} %bitcast.21), calls=%async_computation.3 | async-start | bytes 524288 | tf_op jit(solution)/shard_map/all_to_all | solution.py:117
  86.5 0.9 fusion.46
  87.5 0.9 fusion.6
  88.4 1.0 copy.38
  89.4 7.9 %all-to-all-done.3 = bf16[2,64,2,512]{3,0,2,1:T(2,128)(2,1)S(1)} async-done(((bf16[2,64,2,512]{3,0,2,1:T(2,128)(2,1)}), bf16[2,64,2,512]{3,0,2,1:T(2,128)(2,1)S(1)}, u32[]{:S(2)}, u32[]{:S(2)}) %all-to-all-start.3) | async-done | bytes 262176 | tf_op jit(solution)/shard_map/all_to_all | solution.py:117
  97.3 5.5 %all-to-all-start.4 = ((bf16[2,64,2,512]{3,0,2,1:T(2,128)(2,1)}), bf16[2,64,2,512]{3,0,2,1:T(2,128)(2,1)S(1)}, u32[]{:S(2)}, u32[]{:S(2)}) async-start(bf16[2,64,2,512]{3,0,2,1:T(2,128)(2,1)} %bitcast.25), calls=%async_computation.4 | async-start | bytes 524288 | tf_op jit(solution)/shard_map/all_to_all | solution.py:120
  102.7 0.0 reduce-scatter.2.cloned.1.call-start
  102.8 0.2 convert_bitcast_fusion.1
  103.0 0.4 reshape.157
  103.4 10.8 %all-to-all-done.4 = bf16[2,64,2,512]{3,0,2,1:T(2,128)(2,1)S(1)} async-done(((bf16[2,64,2,512]{3,0,2,1:T(2,128)(2,1)}), bf16[2,64,2,512]{3,0,2,1:T(2,128)(2,1)S(1)}, u32[]{:S(2)}, u32[]{:S(2)}) %all-to-all-start.4) | async-done | bytes 262176 | tf_op jit(solution)/shard_map/all_to_all | solution.py:120
  114.2 0.2 convert_bitcast_fusion
  114.5 0.4 reshape.158
  114.8 0.6 fusion.18
  115.5 0.6 fusion.10
  116.1 0.1 copy.36
  116.2 14.6 %all_to_all.66 = bf16[64,1,2,512]{3,2,1,0:T(2,128)(2,1)S(1)} all-to-all(bf16[64,1,2,512]{3,2,1,0:T(2,128)(2,1)S(1)} %copy.36), channel_id=1, replica_groups=mesh['seq'=64,'chan'=8] {'seq'}, dimensions={0} | all-to-all | bytes 262144 | tf_op jit(solution)/shard_map/all_to_all | solution.py:130
  130.9 0.0 copy-start.1
  131.0 150.8 %all-gather.2.cloned.1.call-done = bf16[512,4096]{0,1:T(8,128)(2,1)} async-done(((bf16[512,64]{0,1:T(8,128)(2,1)}), bf16[512,4096]{0,1:T(8,128)(2,1)}) %all-gather.2.cloned.1.call-update) | async-done | bytes 4194320 | tf_op jit(solution)/shard_map/all_gather | solution.py:141
  281.8 4.7 %convolution_convert_fusion = bf16[128,4096]{1,0:T(8,128)(2,1)} fusion(bf16[128,512]{1,0:T(8,128)(2,1)S(1)} %fusion.26, bf16[512,4096]{0,1:T(8,128)(2,1)} %all-gather.2.cloned.1.call-done), kind=kOutput, calls=%fused_computation | convolution fusion | flops 537395200 | bytes 5373952 | tf_op jit(solution)/shard_map/dot_general | solution.py:139
  286.5 0.0 copy-done.1
  286.5 0.0 reduce-scatter.2.cloned.1.call-update
  286.5 0.3 slice.56
  286.8 79.0 %reduce-scatter.2.cloned.1.call-done = bf16[128,512]{1,0:T(8,128)(2,1)} async-done(((bf16[128,4096]{1,0:T(8,128)(2,1)}), bf16[128,512]{1,0:T(8,128)(2,1)}) %reduce-scatter.2.cloned.1.call-update) | async-done | bytes 131088 | tf_op jit(solution)/shard_map/reduce_scatter | solution.py:144
  365.8 1.6 fusion.27
  (11 shorter events, 0.2 us)
Async XLA Ops:
  7.2 274.6 %all-gather.2.cloned.1.call-start = ((), (), s32[]{:S(2)}) async-start(), calls=%async_computation.7 | async-start | bytes 4259840 | tf_op jit(solution)/shard_map/all_gather | solution.py:141
  7.9 2.2 copy-start.3
  10.1 5.0 %copy-start.2 = (bf16[3,3,512]{2,1,0:T(4,128)(2,1)S(1)}, bf16[3,3,512]{2,1,0:T(4,128)(2,1)}, u32[]{:S(2)}) copy-start(bf16[3,3,512]{2,1,0:T(4,128)(2,1)} %param.7) | copy-start | bytes 27652
  11.0 4.8 %collective-permute-start = (bf16[2,3,512]{2,0,1:T(2,128)(2,1)S(1)}, bf16[2,3,512]{2,0,1:T(2,128)(2,1)S(1)}, u32[]{:S(2)}, u32[]{:S(2)}) collective-permute-start(bf16[2,3,512]{2,0,1:T(2,128)(2,1)S(1)} %copy.43), channel_id=1, source_target_pairs={{0,8},{8,16},{16,24},{24,32},{32,40},{40,48},{48,56},{56,64},{64,7... | collective-permute-start | bytes 18440 | tf_op jit(solution)/shard_map/ppermute | solution.py:12
  17.0 24.2 %all-to-all-start = ((bf16[1,64,2,512]{3,2,0,1:T(2,128)(2,1)}), bf16[1,64,2,512]{3,2,0,1:T(2,128)(2,1)S(1)}, u32[]{:S(2)}, u32[]{:S(2)}) async-start(bf16[1,64,2,512]{3,2,0,1:T(2,128)(2,1)} %bitcast.4), calls=%async_computation | async-start | bytes 262144 | tf_op jit(solution)/shard_map/all_to_all | solution.py:86
  43.4 16.0 %all-to-all-start.2 = ((bf16[128,1,2,512]{3,2,1,0:T(2,128)(2,1)}), bf16[128,1,2,512]{3,2,1,0:T(2,128)(2,1)S(1)}, u32[]{:S(2)}, u32[]{:S(2)}) async-start(bf16[128,1,2,512]{3,2,1,0:T(2,128)(2,1)} %copy.30), calls=%async_computation.2 | async-start | bytes 524288 | tf_op jit(solution)/shard_map/all_to_all | solution.py:101
  59.4 16.6 %all-to-all-start.1 = ((bf16[128,1,2,512]{3,2,1,0:T(2,128)(2,1)}), bf16[128,1,2,512]{3,2,1,0:T(2,128)(2,1)S(1)}, u32[]{:S(2)}, u32[]{:S(2)}) async-start(bf16[128,1,2,512]{3,2,1,0:T(2,128)(2,1)} %copy.28), calls=%async_computation.1 | async-start | bytes 524288 | tf_op jit(solution)/shard_map/all_to_all | solution.py:98
  76.3 2.4 copy-start
  81.6 15.6 %all-to-all-start.3 = ((bf16[2,64,2,512]{3,0,2,1:T(2,128)(2,1)}), bf16[2,64,2,512]{3,0,2,1:T(2,128)(2,1)S(1)}, u32[]{:S(2)}, u32[]{:S(2)}) async-start(bf16[2,64,2,512]{3,0,2,1:T(2,128)(2,1)} %bitcast.21), calls=%async_computation.3 | async-start | bytes 524288 | tf_op jit(solution)/shard_map/all_to_all | solution.py:117
  97.3 17.0 %all-to-all-start.4 = ((bf16[2,64,2,512]{3,0,2,1:T(2,128)(2,1)}), bf16[2,64,2,512]{3,0,2,1:T(2,128)(2,1)S(1)}, u32[]{:S(2)}, u32[]{:S(2)}) async-start(bf16[2,64,2,512]{3,0,2,1:T(2,128)(2,1)} %bitcast.25), calls=%async_computation.4 | async-start | bytes 524288 | tf_op jit(solution)/shard_map/all_to_all | solution.py:120
  102.7 263.1 %reduce-scatter.2.cloned.1.call-start = ((), (), s32[]{:S(2)}) async-start(), calls=%async_computation.8 | async-start | bytes 1179648 | tf_op jit(solution)/shard_map/reduce_scatter | solution.py:144
  130.9 155.5 %copy-start.1 = (bf16[128,512]{1,0:T(8,128)(2,1)}, bf16[128,512]{1,0:T(8,128)(2,1)S(1)}, u32[]{:S(2)}) copy-start(bf16[128,512]{1,0:T(8,128)(2,1)S(1)} %fusion.26) | copy-start | bytes 393220
Sparse Core Ops, SparseCore 0:
  10.1 271.6 all-gather.1
  286.6 79.1 reduce-scatter.1
where the time goes:
time: 376 us; the launch traced here: 374 us
  waiting for transfers between devices  282 us (75%)
  starting transfers between devices  37.8 us (10%)
  blocking collectives  14.6 us (4%)
  between operations  14.4 us (4%)
  matrix products  13.7 us (4%)
  local copies, waits for them, and re-layouts  9.26 us (2%)
    all_gather x1, waiting for transfers between devices, per_device(): lax.all_gather(out_weight, 'seq', axis=1, tiled=True)  151 us
    reduce_scatter x1, waiting for transfers between devices, per_device(): lax.psum_scatter(partial_value.astype(jnp.bfloat16), 'chan', scatter_dime...  79 us
    all_to_all x1, blocking collectives, per_device(): lax.all_to_all(result.reshape(devices, 1, slab_rows, channels).astype(jnp...  14.6 us
    all_to_all x1, starting transfers between devices, per_device(): lax.all_to_all(pieces, 'seq', split_axis=1, concat_axis=0, tiled=True)  13.7 us
    all_to_all x1, waiting for transfers between devices, per_device(): lax.all_to_all(sent[0].astype(jnp.bfloat16), 'seq', split_axis=0, concat_...  11.3 us
    all_to_all x1, waiting for transfers between devices, per_device(): lax.all_to_all(returned[1].astype(jnp.bfloat16), 'seq', split_axis=1, con...  10.8 us
    all_to_all x1, waiting for transfers between devices, per_device(): lax.all_to_all(sent[1].astype(jnp.bfloat16), 'seq', split_axis=0, concat_...  10.4 us
    all_to_all x1, waiting for transfers between devices, per_device(): lax.all_to_all(pieces, 'seq', split_axis=1, concat_axis=0, tiled=True)  10.4 us
  transfers between devices with their start and end apart: 8, of which 8 were waited for; matrix products, arithmetic and copies ran while one was open for 5% of the time, Pallas kernels for 0%

commit v1 on v0

v1 whole, which is shorter than its diff:
```python
import jax
import jax.numpy as jnp
import numpy as np
from jax import lax
from jax.experimental import pallas as pl
from jax.experimental.pallas import tpu as pltpu
from jax.sharding import PartitionSpec as P

MESH = pl.DeviceIdType.MESH
F32 = jnp.float32
BF16 = jnp.bfloat16

NX, NZ, NY = 4, 2, 8
NH = 4
SEQ = NX * NZ * NY
TOK = 128
CH = 512
OWN = CH // SEQ
LEN = 2 * SEQ * TOK
FAR_FIRST = (4, 3, 5, 2, 6, 1, 7)


def tables():
    a = np.concatenate([np.arange(0, 128, 2), np.arange(1, 128, 2)])
    p = np.arange(SEQ)
    m = np.arange(TOK)
    t1 = 2 * np.pi * (np.outer(a, p) % 128) / 128
    first = np.concatenate([np.cos(t1), -np.sin(t1)], 0)
    hi = first.astype(jnp.bfloat16)
    lo = (first - hi.astype(np.float64)).astype(jnp.bfloat16)
    first = np.concatenate([hi, lo], 1)
    tw = 2 * np.pi * (np.outer(a, m) % LEN) / LEN
    twid = np.stack([np.cos(tw), np.sin(tw)]).astype(np.float32)
    t2 = 2 * np.pi * (np.outer(m, m) % 128) / 128
    c2, s2 = np.cos(t2), np.sin(t2)
    forward = np.block([[c2, -s2], [s2, c2]]).astype(jnp.bfloat16)
    inverse = np.block([[c2, s2], [-s2, c2]]).astype(jnp.bfloat16)
    last = (np.concatenate([np.cos(t1), -np.sin(t1)], 0).T / LEN).astype(jnp.bfloat16)
    return first, twid, forward, inverse, last


def kernel(
    ids, tab, taps, spec, wt, first, twid, forward, inverse, last,
    mixed, gated,
    ids_in, spec_out, spec_in, spec_f, ext, sig_out, sig_in, conv_out, conv_in,
    gat, wg, part, pair_out, pair_in, red_out, red_in,
    s_ids, s_spec, s_sig, s_conv, s_wy, s_wx, s_gat, s_pair, s_red,
):
    seq = lax.axis_index("seq")
    chan = lax.axis_index("chan")
    x, zl, y = seq // (NZ * NY), lax.rem(seq // NY, NZ), lax.rem(seq, NY)
    zh, co = chan // 2, lax.rem(chan, 2)

    def seq_at(px, pz, py):
        return px * (NZ * NY) + pz * NY + py

    def peer(k):
        return seq_at(
            lax.rem(x + k // (NZ * NY), NX),
            lax.rem(zl + lax.rem(k // NY, NZ), NZ),
            lax.rem(y + lax.rem(k, NY), NY),
        )

    def remote(src, dst, sems, device):
        return pltpu.make_async_remote_copy(
            src_ref=src, dst_ref=dst, send_sem=sems.at[0], recv_sem=sems.at[1],
            device_id=device, device_id_type=MESH,
        )

    other_core = {"chan": zh * 2 + 1 - co}
    other_z = {"seq": seq_at(x, 1 - zl, y)}
    own_sum = jnp.logical_and(co == zl, zh // 2 == co)

    barrier = pltpu.get_barrier_semaphore()

    def greet(k, _):
        pl.semaphore_signal(barrier, inc=1, device_id={"seq": peer(k)}, device_id_type=MESH)
        return 0

    lax.fori_loop(1, SEQ, greet, 0)
    pl.semaphore_signal(barrier, inc=1, device_id=other_core, device_id_type=MESH)
    for h in range(NH):
        @pl.when(jnp.logical_not(jnp.logical_and(own_sum, zh == h)))
        def _():
            source = {"seq": seq_at(x, co, y), "chan": h * 2 + zh // 2}
            pl.semaphore_signal(barrier, inc=1, device_id=source, device_id_type=MESH)

    for r in range(2):
        for j in range(CH // 128):
            cols = pl.ds(j * 128, 128)
            pieces = [
                spec[r, a, :, cols].astype(F32).T.reshape(128 // OWN, OWN, 128) for a in range(2)
            ]
            spec_out[pl.ds(j * (128 // OWN), 128 // OWN), pl.ds(r * 16, 16), :] = (
                jnp.concatenate(pieces, 1).astype(BF16)
            )

    pl.semaphore_wait(barrier, SEQ - 1 + 1 + NH - own_sum.astype(jnp.int32))

    ids_copy = remote(ids, ids_in, s_ids, {"seq": lax.rem(seq + 1, SEQ)})
    ids_copy.start()

    def send_all(src, dst, sems):
        def one(k, _):
            d = peer(k)
            remote(src.at[d], dst.at[seq], sems, {"seq": d}).start()
            return 0

        lax.fori_loop(1, SEQ, one, 0)

    def wait_all(src, dst, sems):
        some = pl.ds(0, SEQ - 1)
        copy = remote(src.at[some], dst.at[some], sems, other_z)
        copy.wait_recv()
        copy.wait_send()

    for k in FAR_FIRST:
        remote(
            wt, wg.at[x, y], s_wy, {"seq": seq_at(x, zl, lax.rem(y + k, NY))}
        ).start()
    send_all(spec_out, spec_in, s_spec)
    wg[pl.ds(x, 1), pl.ds(y, 1)] = wt[...][None, None]
    spec_in[pl.ds(seq, 1)] = spec_out[pl.ds(seq, 1)]

    vocab = lax.broadcasted_iota(jnp.int32, (tab.shape[0], TOK), 0)

    def one_hot(row):
        return jnp.where(vocab == row[...], 1.0, 0.0).astype(F32).T.astype(BF16)

    hot = one_hot(ids)
    for g in range(4):
        cols = pl.ds(g * CH, CH)
        ext[g, pl.ds(8, TOK), :] = jnp.dot(hot, tab[:, cols], preferred_element_type=F32)
    ids_copy.wait_recv()
    before = one_hot(ids_in)[TOK - 16 :, :]
    inside = jnp.where(seq > 0, 1.0, 0.0).astype(F32)
    for g in range(3):
        cols = pl.ds(g * CH, CH)
        halo = jnp.dot(before, tab[:, cols], preferred_element_type=F32)
        ext[g, pl.ds(0, 8), :] = halo[8:, :] * inside

    def shortened(g):
        weights = taps[g].astype(F32)
        out = weights[0:1] * ext[g, pl.ds(8, TOK), :]
        out = out + weights[1:2] * ext[g, pl.ds(7, TOK), :]
        return out + weights[2:3] * ext[g, pl.ds(6, TOK), :]

    signal = (shortened(1) * shortened(2)).astype(BF16).astype(F32)
    for j in range(CH // 128):
        block = signal[:, j * 128 : (j + 1) * 128].T
        n = 128 // OWN
        sig_out[pl.ds(j * n, n)] = block.reshape(n, OWN, TOK)
    send_all(sig_out, sig_in, s_sig)
    sig_in[pl.ds(seq, 1)] = sig_out[pl.ds(seq, 1)]

    some = pl.ds(0, NY - 1)
    wy = remote(wg.at[0, some], wg.at[0, some], s_wy, other_z)
    wy.wait_recv()
    for k in (2, 1, 3):
        remote(
            wg.at[x], wg.at[x], s_wx, {"seq": seq_at(lax.rem(x + k, NX), zl, y)}
        ).start()

    wait_all(spec_out, spec_in, s_spec)
    spec_f[...] = spec_in[...].astype(F32)
    wait_all(sig_out, sig_in, s_sig)
    cos, sin = twid[0], twid[1]
    for c in range(OWN):
        s = sig_in[:, c, :].astype(BF16)
        z = jnp.dot(first[...], jnp.concatenate([s, s], 0), preferred_element_type=F32)
        zr, zi = z[:128], z[128:]
        z = jnp.concatenate([zr * cos + zi * sin, zi * cos - zr * sin], 1).astype(BF16)
        f = jnp.dot(z, forward[...], preferred_element_type=F32)
        fr, fi = f[:, :128], f[:, 128:]
        hr = jnp.concatenate([spec_f[:, c, :], spec_f[:, 8 + c, :]], 0)
        hi = jnp.concatenate([spec_f[:, 16 + c, :], spec_f[:, 24 + c, :]], 0)
        f = jnp.concatenate([fr * hr - fi * hi, fr * hi + fi * hr], 1).astype(BF16)
        b = jnp.dot(f, inverse[...], preferred_element_type=F32)
        br, bi = b[:, :128], b[:, 128:]
        b = jnp.concatenate([br * cos - bi * sin, bi * cos + br * sin], 0).astype(BF16)
        conv_out[:, c, :] = jnp.dot(last[...], b, preferred_element_type=F32)
    send_all(conv_out, conv_in, s_conv)
    conv_in[pl.ds(seq, 1)] = conv_out[pl.ds(seq, 1)]

    query = shortened(0)
    wait_all(conv_out, conv_in, s_conv)
    for j in range(CH // 128):
        n = 128 // OWN
        block = conv_in[pl.ds(j * n, n)].reshape(128, TOK).T
        value = (query[:, j * 128 : (j + 1) * 128] * block).astype(BF16)
        gated[:, pl.ds(j * 128, 128)] = value
        gat[pl.ds(zl, 1), :, pl.ds(j * 128, 128)] = value[None]
    gat_copy = remote(gat.at[zl], gat.at[zl], s_gat, other_z)
    gat_copy.start()

    some = pl.ds(0, NX - 1)
    wx = remote(wg.at[some], wg.at[some], s_wx, other_z)
    wx.wait_recv()
    for turn in range(2):
        t = zl if turn == 0 else 1 - zl
        if turn == 1:
            gat_copy.wait_recv()
        rows = gat[t]

        def project(block):
            weights = wg[block].reshape(NY * 64, CH)
            return lax.dot_general(
                rows, weights, (((1,), (1,)), ((), ())), preferred_element_type=F32
            )

        for i in range(2):
            pair_out[turn, i] = project(2 * (1 - co) + i).astype(BF16)
        pair_copy = remote(pair_out.at[turn], pair_in.at[turn], s_pair.at[turn], other_core)
        pair_copy.start()
        for i in range(2):
            part[turn, i] = project(2 * co + i)
        pair_copy.wait_recv()
        for i in range(2):
            red_out[turn, i] = (part[turn, i] + pair_in[turn, i].astype(F32)).astype(BF16)

        for i in range(2):
            to = {"seq": seq_at(x, t, y), "chan": (2 * co + i) * 2 + zl}
            copy = remote(red_out.at[turn, i], red_in.at[zh], s_red, to)
            if turn == 1:
                copy.start()
                continue

            own = jnp.logical_and(own_sum, 2 * co + i == zh)

            @pl.when(own)
            def _():
                red_in[pl.ds(zh, 1)] = red_out[0, pl.ds(i, 1)]

            @pl.when(jnp.logical_not(own))
            def _():
                copy.start()

    for count in (NH - 1, NH):
        @pl.when(own_sum == (count == NH - 1))
        def _():
            some = pl.ds(0, count)
            copy = remote(red_in.at[some], red_in.at[some], s_red, other_z)
            copy.wait_recv()
            copy.wait_send()

    total = ext[3, pl.ds(8, TOK), :]
    for h in range(NH):
        total = total + red_in[h].astype(F32)
    mixed[...] = total.astype(BF16)

    ids_copy.wait_send()
    wy.wait_send()
    wx.wait_send()
    gat_copy.wait_send()
    for turn in range(2):
        remote(pair_out.at[turn], pair_in.at[turn], s_pair.at[turn], other_core).wait_send()


def per_device(token_ids, vocab_table, short_taps, filter_spec, out_weight):
    first, twid, forward, inverse, last = tables()
    vmem = pl.BlockSpec(memory_space=pltpu.VMEM)
    out = jax.ShapeDtypeStruct((TOK, CH), BF16)
    args = (
        token_ids.reshape(1, TOK),
        vocab_table.reshape(vocab_table.shape[0], 4 * CH),
        short_taps,
        filter_spec,
        out_weight.T,
        first, twid, forward, inverse, last,
    )
    args = tuple(jnp.asarray(arg) for arg in args)
    dma2 = pltpu.SemaphoreType.DMA((2,))
    return pl.pallas_call(
        kernel,
        out_shape=(out, out),
        in_specs=[vmem] * len(args),
        out_specs=(vmem, vmem),
        scratch_shapes=[
            pltpu.VMEM((1, TOK), jnp.int32),
            pltpu.VMEM((SEQ, 32, 128), BF16),
            pltpu.VMEM((SEQ, 32, 128), BF16),
            pltpu.VMEM((SEQ, 32, 128), F32),
            pltpu.VMEM((4, 8 + TOK, CH), F32),
            pltpu.VMEM((SEQ, OWN, TOK), F32),
            pltpu.VMEM((SEQ, OWN, TOK), F32),
            pltpu.VMEM((SEQ, OWN, TOK), F32),
            pltpu.VMEM((SEQ, OWN, TOK), F32),
            pltpu.VMEM((NZ, TOK, CH), BF16),
            pltpu.VMEM((NX, NY, 64, CH), BF16),
            pltpu.VMEM((2, 2, TOK, CH), F32),
            pltpu.VMEM((2, 2, TOK, CH), BF16),
            pltpu.VMEM((2, 2, TOK, CH), BF16),
            pltpu.VMEM((2, 2, TOK, CH), BF16),
            pltpu.VMEM((NH, TOK, CH), BF16),
            dma2, dma2, dma2, dma2, dma2, dma2, dma2,
            pltpu.SemaphoreType.DMA((2, 2)),
            dma2,
        ],
        compiler_params=pltpu.CompilerParams(
            collective_id=0, has_side_effects=True, vmem_limit_bytes=48 << 20
        ),
        name="hyena",
    )(*args)


def solution(mesh):
    placed = (
        P("seq"),
        P(None, None, "chan"),
        P(None, None, "chan"),
        P(None, "seq", None, "chan"),
        P("chan", "seq"),
    )
    return jax.shard_map(
        per_device,
        mesh=mesh,
        in_specs=placed,
        out_specs=(P("seq", "chan"), P("seq", "chan")),
        check_vma=False,
    )
```

time: 376 us -> 87.5 us (0.23)
  waiting for transfers between devices: 282 us -> 0 us
  Pallas kernels: 0 us -> 83 us
  starting transfers between devices: 37.8 us -> 0 us
  blocking collectives: 14.6 us -> 0 us
  matrix products: 13.7 us -> 0 us
  between operations: 14.4 us -> 0.79 us
  local copies, waits for them, and re-layouts: 9.26 us -> 3.64 us
    all_gather x1 -> x0, waiting for transfers between devices: 151 us -> none  [per_device(): lax.all_gather(out_weight, 'seq', axis=1, tiled=True)]
    pallas_call x0 -> x1, Pallas kernels: none -> 83 us  [per_device(): pl.pallas_call(kernel, out_shape=(out, out), in_specs=[vmem] * len(args),...]
    reduce_scatter x1 -> x0, waiting for transfers between devices: 79 us -> none  [per_device(): lax.psum_scatter(partial_value.astype(jnp.bfloat16), 'chan', scatter_dime...]
    all_to_all x5 -> x0, waiting for transfers between devices: 50.8 us -> none  [the longest x1 11.3 us: per_device(): lax.all_to_all(sent[0].astype(jnp.bfloat16), 'seq', split_axis=0, concat_...]
    all_to_all x5 -> x0, starting transfers between devices: 33.7 us -> none  [the longest x1 13.7 us: per_device(): lax.all_to_all(pieces, 'seq', split_axis=1, concat_axis=0, tiled=True)]
    all_to_all x1 -> x0, blocking collectives: 14.6 us -> none  [per_device(): lax.all_to_all(result.reshape(devices, 1, slab_rows, channels).astype(jnp...]
    dot_general x14 -> x0, matrix products: 13.7 us -> none  [the longest x12 8.51 us: contract(): jnp.einsum(pattern, operand, table, precision=lax.Precision.HIGHEST, pref...]
    convert_element_type x11 -> x0, local copies, waits for them, and re-layouts: 5.66 us -> none  [the longest x1 1 us: per_device(): returned[0].astype(jnp.bfloat16)]
  transfers between devices with their start and end apart: 8 -> 0, of which waited for: 8 -> 0; matrix products, arithmetic and copies ran while one was open for 5% -> 0% of each run, Pallas kernels for 0% -> 0%
where the time goes in v1:
time: 87.5 us; the launch traced here: 87.4 us
  Pallas kernels  83 us (95%)
  local copies, waits for them, and re-layouts  3.64 us (4%)
    pallas_call x1, Pallas kernels, per_device(): pl.pallas_call(kernel, out_shape=(out, out), in_specs=[vmem] * len(args),...  83 us
    unnamed x21, local copies, waits for them, and re-layouts  3.64 us

profile of v1, /device:TPU:1, one launch (start us, length us, event | category | flops | bytes accessed | tf_op | source)
XLA Modules:
  0.0 87.4 jit_solution(12153328501802460108)
XLA Ops:
  0.6 0.0 copy-start
  0.6 0.0 copy-start.1
  0.7 0.0 copy-start.2
  0.7 0.0 copy-start.3
  0.7 0.0 copy-start.4
  0.7 0.0 copy-start.5
  0.7 0.0 copy-start.6
  0.7 0.0 copy-start.7
  0.7 0.0 copy-start.8
  0.7 2.3 %copy.12 = bf16[64,8,4,512]{3,1,2,0:T(8,128)(2,1)S(1)} copy(bf16[64,8,4,512]{3,2,1,0:T(4,128)(2,1)} %bitcast.7) | data formatting | bytes 4194304
  3.0 0.0 copy-done
  3.0 0.0 copy-done.1
  3.0 0.0 copy-done.2
  3.0 0.0 copy-done.3
  3.1 0.0 copy-done.4
  3.1 0.0 copy-done.5
  3.1 0.0 copy-done.6
  3.1 0.0 copy-done.7
  3.1 0.0 copy-done.8
  3.1 83.0 %hyena.1 = (bf16[128,512]{1,0:T(8,128)(2,1)S(1)}, bf16[128,512]{1,0:T(8,128)(2,1)S(1)}) custom-call(s32[1,128]{1,0:T(1,128)S(1)} %bitcast.6, bf16[512,2048]{1,0:T(8,128)(2,1)S(1)} %bitcast.4, bf16[3,3,512]{2,1,0:T(4,128)(2,1)S(1)} %copy-done.7, bf16[2,2,128,512]{3,2,1,0:T(8,128)(2,1)S(1)} %copy-done, bf16[64,512]{1,0:T(8,128)(2,1)S(1)} %bitcast.5, ...), custom_call_target="tpu_custom_call" | custom-call | tf_op jit(solution)/shard_map/hyena/pallas_call | solution.py:273
  86.1 0.7 copy.15
  86.7 0.7 copy.16
Async XLA Ops:
  0.6 2.4 %copy-start = (bf16[2,2,128,512]{3,2,1,0:T(8,128)(2,1)S(1)}, bf16[2,2,128,512]{3,2,1,0:T(8,128)(2,1)}, u32[]{:S(2)}) copy-start(bf16[2,2,128,512]{3,2,1,0:T(8,128)(2,1)} %spec.1) | copy-start | bytes 1572868
  0.6 2.4 %copy-start.1 = (bf16[256,256]{1,0:T(8,128)(2,1)S(1)}, bf16[256,256]{1,0:T(8,128)(2,1)}, u32[]{:S(2)}) copy-start(bf16[256,256]{1,0:T(8,128)(2,1)} %constant.13.clone.inverse) | copy-start | bytes 393220
  0.7 2.4 %copy-start.2 = (bf16[256,256]{1,0:T(8,128)(2,1)S(1)}, bf16[256,256]{1,0:T(8,128)(2,1)}, u32[]{:S(2)}) copy-start(bf16[256,256]{1,0:T(8,128)(2,1)} %constant.12.clone.forward) | copy-start | bytes 393220
  0.7 2.4 %copy-start.3 = (f32[2,128,128]{2,1,0:T(8,128)S(1)}, f32[2,128,128]{2,1,0:T(8,128)}, u32[]{:S(2)}) copy-start(f32[2,128,128]{2,1,0:T(8,128)} %constant.11.clone.twid) | copy-start | bytes 393220
  0.7 2.4 %copy-start.4 = (bf16[512,64]{0,1:T(8,128)(2,1)S(1)}, bf16[512,64]{0,1:T(8,128)(2,1)}, u32[]{:S(2)}) copy-start(bf16[512,64]{0,1:T(8,128)(2,1)} %param.14) | copy-start | bytes 196612
  0.7 2.4 %copy-start.5 = (bf16[256,128]{1,0:T(8,128)(2,1)S(1)}, bf16[256,128]{1,0:T(8,128)(2,1)}, u32[]{:S(2)}) copy-start(bf16[256,128]{1,0:T(8,128)(2,1)} %constant.10.clone.first) | copy-start | bytes 196612
  0.7 2.4 %copy-start.6 = (bf16[64,256]{1,0:T(8,128)(2,1)S(1)}, bf16[64,256]{1,0:T(8,128)(2,1)}, u32[]{:S(2)}) copy-start(bf16[64,256]{1,0:T(8,128)(2,1)} %constant.14.clone.last) | copy-start | bytes 98308
  0.7 2.4 %copy-start.7 = (bf16[3,3,512]{2,1,0:T(4,128)(2,1)S(1)}, bf16[3,3,512]{2,1,0:T(4,128)(2,1)}, u32[]{:S(2)}) copy-start(bf16[3,3,512]{2,1,0:T(4,128)(2,1)} %taps.1) | copy-start | bytes 27652
  0.7 2.4 %copy-start.8 = (s32[128]{0:T(128)S(1)}, s32[128]{0:T(128)}, u32[]{:S(2)}) copy-start(s32[128]{0:T(128)} %param.10) | copy-start | bytes 1540

commit v2 on v1

--- a/solution.py
+++ b/solution.py
@@ -17,7 +17,7 @@
 CH = 512
 OWN = CH // SEQ
 LEN = 2 * SEQ * TOK
-FAR_FIRST = (4, 3, 5, 2, 6, 1, 7)
+NEAR_FIRST = (1, 7, 2, 6, 3, 5, 4)
 
 
 def tables():
@@ -43,8 +43,8 @@
     ids, tab, taps, spec, wt, first, twid, forward, inverse, last,
     mixed, gated,
     ids_in, spec_out, spec_in, spec_f, ext, sig_out, sig_in, conv_out, conv_in,
-    gat, wg, part, pair_out, pair_in, red_out, red_in,
-    s_ids, s_spec, s_sig, s_conv, s_wy, s_wx, s_gat, s_pair, s_red,
+    gat, wy, wg, red_out, red_in,
+    s_ids, s_spec, s_sig, s_conv, s_wy, s_wyr, s_wx, s_wl, s_gat, s_red,
 ):
     seq = lax.axis_index("seq")
     chan = lax.axis_index("chan")
@@ -78,7 +78,9 @@
         return 0
 
     lax.fori_loop(1, SEQ, greet, 0)
-    pl.semaphore_signal(barrier, inc=1, device_id=other_core, device_id_type=MESH)
+    for k in range(NX):
+        beside = {"seq": seq_at(lax.rem(x + k, NX), zl, y), "chan": zh * 2 + 1 - co}
+        pl.semaphore_signal(barrier, inc=1, device_id=beside, device_id_type=MESH)
     for h in range(NH):
         @pl.when(jnp.logical_not(jnp.logical_and(own_sum, zh == h)))
         def _():
@@ -95,7 +97,16 @@
                 jnp.concatenate(pieces, 1).astype(BF16)
             )
 
-    pl.semaphore_wait(barrier, SEQ - 1 + 1 + NH - own_sum.astype(jnp.int32))
+    vocab = lax.broadcasted_iota(jnp.int32, (tab.shape[0], TOK), 0)
+
+    def one_hot(row):
+        return jnp.where(vocab == row[...], 1.0, 0.0).astype(F32).T.astype(BF16)
+
+    hot = one_hot(ids)
+    for g in range(4):
+        cols = pl.ds(g * CH, CH)
+        ext[g, pl.ds(8, TOK), :] = jnp.dot(hot, tab[:, cols], preferred_element_type=F32)
+    pl.semaphore_wait(barrier, SEQ - 1 + NX + NH - own_sum.astype(jnp.int32))
 
     ids_copy = remote(ids, ids_in, s_ids, {"seq": lax.rem(seq + 1, SEQ)})
     ids_copy.start()
@@ -114,23 +125,50 @@
         copy.wait_recv()
         copy.wait_send()
 
-    for k in FAR_FIRST:
-        remote(
-            wt, wg.at[x, y], s_wy, {"seq": seq_at(x, zl, lax.rem(y + k, NY))}
-        ).start()
+    ahead = 1 - 2 * co
+    keeps = co == x // 2
+
+    def row_of(k):
+        return lax.rem(y + NY + ahead * k, NY)
+
+    def along_y(block, way):
+        return pltpu.make_async_remote_copy(
+            src_ref=wy.at[block], dst_ref=wy.at[block],
+            send_sem=s_wy.at[0], recv_sem=s_wyr.at[block],
+            device_id={"seq": seq_at(x, zl, row_of(way))}, device_id_type=MESH,
+        )
+
+    def along_x(block):
+        slot = wg.at[2 * co + lax.rem(x, 2), block]
+        for k in (2, 1, 3):
+            to = {"seq": seq_at(lax.rem(x + k, NX), zl, y), "chan": zh * 2 + x // 2}
+            remote(wy.at[block], slot, s_wx, to).start()
+
+        @pl.when(keeps)
+        def _():
+            pltpu.make_async_copy(wy.at[block], slot, s_wl).start()
+
+        @pl.when(jnp.logical_not(keeps))
+        def _():
+            remote(wy.at[block], slot, s_wx, other_core).start()
+
+    def weights_step(step):
+        for way in (1, -1):
+            if step > NY // 2 - (way < 0):
+                continue
+            along_y(row_of(-way * step), way).wait_recv()
+            if step < NY // 2 - (way < 0):
+                along_y(row_of(-way * step), way).start()
+            along_x(row_of(-way * step))
+
+    wy[pl.ds(y, 1)] = wt[...][None]
+    along_y(y, 1).start()
+    along_y(y, -1).start()
+    along_x(y)
     send_all(spec_out, spec_in, s_spec)
-    wg[pl.ds(x, 1), pl.ds(y, 1)] = wt[...][None, None]
     spec_in[pl.ds(seq, 1)] = spec_out[pl.ds(seq, 1)]
-
-    vocab = lax.broadcasted_iota(jnp.int32, (tab.shape[0], TOK), 0)
-
-    def one_hot(row):
-        return jnp.where(vocab == row[...], 1.0, 0.0).astype(F32).T.astype(BF16)
-
-    hot = one_hot(ids)
-    for g in range(4):
-        cols = pl.ds(g * CH, CH)
-        ext[g, pl.ds(8, TOK), :] = jnp.dot(hot, tab[:, cols], preferred_element_type=F32)
+    weights_step(1)
+
     ids_copy.wait_recv()
     before = one_hot(ids_in)[TOK - 16 :, :]
     inside = jnp.where(seq > 0, 1.0, 0.0).astype(F32)
@@ -153,16 +191,11 @@
     send_all(sig_out, sig_in, s_sig)
     sig_in[pl.ds(seq, 1)] = sig_out[pl.ds(seq, 1)]
 
-    some = pl.ds(0, NY - 1)
-    wy = remote(wg.at[0, some], wg.at[0, some], s_wy, other_z)
-    wy.wait_recv()
-    for k in (2, 1, 3):
-        remote(
-            wg.at[x], wg.at[x], s_wx, {"seq": seq_at(lax.rem(x + k, NX), zl, y)}
-        ).start()
-
+    weights_step(2)
+    weights_step(3)
     wait_all(spec_out, spec_in, s_spec)
     spec_f[...] = spec_in[...].astype(F32)
+    weights_step(4)
     wait_all(sig_out, sig_in, s_sig)
     cos, sin = twid[0], twid[1]
     for c in range(OWN):
@@ -189,49 +222,53 @@
         block = conv_in[pl.ds(j * n, n)].reshape(128, TOK).T
         value = (query[:, j * 128 : (j + 1) * 128] * block).astype(BF16)
         gated[:, pl.ds(j * 128, 128)] = value
-        gat[pl.ds(zl, 1), :, pl.ds(j * 128, 128)] = value[None]
-    gat_copy = remote(gat.at[zl], gat.at[zl], s_gat, other_z)
-    gat_copy.start()
-
-    some = pl.ds(0, NX - 1)
-    wx = remote(wg.at[some], wg.at[some], s_wx, other_z)
-    wx.wait_recv()
+        gat[pl.ds(zl, 1), pl.ds(co, 1), :, pl.ds(j * 128, 128)] = value[None, None]
+    own = gat.at[zl, co]
+    to_core = remote(own, own, s_gat.at[0], other_core)
+    to_core.start()
+    to_z = remote(own, own, s_gat.at[1], other_z)
+    to_z.start()
+
+    for count in (3, 4):
+        @pl.when(keeps == (count == 3))
+        def _():
+            some = pl.ds(0, count)
+            remote(wg.at[some], wg.at[some], s_wx, other_z).wait_recv()
+
+    @pl.when(keeps)
+    def _():
+        pltpu.make_async_copy(wy, wg.at[2 * co + lax.rem(x, 2)], s_wl).wait()
+
+    to_core.wait_recv()
     for turn in range(2):
         t = zl if turn == 0 else 1 - zl
         if turn == 1:
-            gat_copy.wait_recv()
-        rows = gat[t]
-
-        def project(block):
-            weights = wg[block].reshape(NY * 64, CH)
-            return lax.dot_general(
-                rows, weights, (((1,), (1,)), ((), ())), preferred_element_type=F32
-            )
-
+            to_z.wait_recv()
+            own = gat.at[1 - zl, co]
+            on = remote(own, own, s_gat.at[2], other_core)
+            on.start()
+            on.wait_recv()
         for i in range(2):
-            pair_out[turn, i] = project(2 * (1 - co) + i).astype(BF16)
-        pair_copy = remote(pair_out.at[turn], pair_in.at[turn], s_pair.at[turn], other_core)
-        pair_copy.start()
-        for i in range(2):
-            part[turn, i] = project(2 * co + i)
-        pair_copy.wait_recv()
-        for i in range(2):
-            red_out[turn, i] = (part[turn, i] + pair_in[turn, i].astype(F32)).astype(BF16)
-
-        for i in range(2):
+            total = jnp.zeros((TOK, CH), F32)
+            for c in range(2):
+                total = total + lax.dot_general(
+                    gat[t, c], wg[2 * c + i].reshape(NY * 64, CH), (((1,), (1,)), ((), ())),
+                    preferred_element_type=F32,
+                )
+            red_out[turn, i] = total.astype(BF16)
             to = {"seq": seq_at(x, t, y), "chan": (2 * co + i) * 2 + zl}
             copy = remote(red_out.at[turn, i], red_in.at[zh], s_red, to)
             if turn == 1:
                 copy.start()
                 continue
 
-            own = jnp.logical_and(own_sum, 2 * co + i == zh)
-
-            @pl.when(own)
+            own_block = jnp.logical_and(own_sum, 2 * co + i == zh)
+
+            @pl.when(own_block)
             def _():
                 red_in[pl.ds(zh, 1)] = red_out[0, pl.ds(i, 1)]
 
-            @pl.when(jnp.logical_not(own))
+            @pl.when(jnp.logical_not(own_block))
             def _():
                 copy.start()
 
@@ -249,11 +286,17 @@
     mixed[...] = total.astype(BF16)
 
     ids_copy.wait_send()
-    wy.wait_send()
-    wx.wait_send()
-    gat_copy.wait_send()
-    for turn in range(2):
-        remote(pair_out.at[turn], pair_in.at[turn], s_pair.at[turn], other_core).wait_send()
+    some = pl.ds(0, NY - 1)
+    remote(wy.at[some], wy.at[some], s_wy, other_z).wait_send()
+    for count in (3, 4):
+        @pl.when(keeps == (count == 3))
+        def _():
+            some = pl.ds(0, count)
+            remote(wg.at[some], wg.at[some], s_wx, other_z).wait_send()
+
+    to_core.wait_send()
+    to_z.wait_send()
+    on.wait_send()
 
 
 def per_device(token_ids, vocab_table, short_taps, filter_spec, out_weight):
@@ -285,15 +328,16 @@
             pltpu.VMEM((SEQ, OWN, TOK), F32),
             pltpu.VMEM((SEQ, OWN, TOK), F32),
             pltpu.VMEM((SEQ, OWN, TOK), F32),
-            pltpu.VMEM((NZ, TOK, CH), BF16),
-            pltpu.VMEM((NX, NY, 64, CH), BF16),
-            pltpu.VMEM((2, 2, TOK, CH), F32),
-            pltpu.VMEM((2, 2, TOK, CH), BF16),
-            pltpu.VMEM((2, 2, TOK, CH), BF16),
+            pltpu.VMEM((NZ, 2, TOK, CH), BF16),
+            pltpu.VMEM((NY, 64, CH), BF16),
+            pltpu.VMEM((4, NY, 64, CH), BF16),
             pltpu.VMEM((2, 2, TOK, CH), BF16),
             pltpu.VMEM((NH, TOK, CH), BF16),
-            dma2, dma2, dma2, dma2, dma2, dma2, dma2,
-            pltpu.SemaphoreType.DMA((2, 2)),
+            dma2, dma2, dma2, dma2, dma2,
+            pltpu.SemaphoreType.DMA((NY,)),
+            dma2,
+            pltpu.SemaphoreType.DMA,
+            pltpu.SemaphoreType.DMA((3, 2)),
             dma2,
         ],
         compiler_params=pltpu.CompilerParams(

time: 87.5 us -> 74.6 us (0.85)
  Pallas kernels: 83 us -> 69.5 us
    pallas_call x1, Pallas kernels: 83 us -> 69.5 us  [per_device(): pl.pallas_call(kernel, out_shape=(out, out), in_specs=[vmem] * len(args),...]
where the time goes in v2:
time: 74.6 us; the launch traced here: 73.9 us
  Pallas kernels  69.5 us (93%)
  local copies, waits for them, and re-layouts  3.64 us (5%)
  between operations  0.79 us (1%)
    pallas_call x1, Pallas kernels, per_device(): pl.pallas_call(kernel, out_shape=(out, out), in_specs=[vmem] * len(args),...  69.5 us
    unnamed x21, local copies, waits for them, and re-layouts  3.64 us

profile of v2, /device:TPU:1, one launch (start us, length us, event | category | flops | bytes accessed | tf_op | source)
XLA Modules:
  0.0 73.9 jit_solution(14286369725793655345)
XLA Ops:
  0.6 0.0 copy-start
  0.6 0.0 copy-start.1
  0.7 0.0 copy-start.2
  0.7 0.0 copy-start.3
  0.7 0.0 copy-start.4
  0.7 0.0 copy-start.5
  0.7 0.0 copy-start.6
  0.7 0.0 copy-start.7
  0.7 0.0 copy-start.8
  0.7 2.3 %copy.12 = bf16[64,8,4,512]{3,1,2,0:T(8,128)(2,1)S(1)} copy(bf16[64,8,4,512]{3,2,1,0:T(4,128)(2,1)} %bitcast.7) | data formatting | bytes 4194304
  3.0 0.0 copy-done
  3.0 0.0 copy-done.1
  3.0 0.0 copy-done.2
  3.0 0.0 copy-done.3
  3.1 0.0 copy-done.4
  3.1 0.0 copy-done.5
  3.1 0.0 copy-done.6
  3.1 0.0 copy-done.7
  3.1 0.0 copy-done.8
  3.1 69.5 %hyena.1 = (bf16[128,512]{1,0:T(8,128)(2,1)S(1)}, bf16[128,512]{1,0:T(8,128)(2,1)S(1)}) custom-call(s32[1,128]{1,0:T(1,128)S(1)} %bitcast.6, bf16[512,2048]{1,0:T(8,128)(2,1)S(1)} %bitcast.4, bf16[3,3,512]{2,1,0:T(4,128)(2,1)S(1)} %copy-done.7, bf16[2,2,128,512]{3,2,1,0:T(8,128)(2,1)S(1)} %copy-done, bf16[64,512]{1,0:T(8,128)(2,1)S(1)} %bitcast.5, ...), custom_call_target="tpu_custom_call" | custom-call | tf_op jit(solution)/shard_map/hyena/pallas_call | solution.py:316
  72.6 0.7 copy.15
  73.3 0.7 copy.16
Async XLA Ops:
  0.6 2.4 %copy-start = (bf16[2,2,128,512]{3,2,1,0:T(8,128)(2,1)S(1)}, bf16[2,2,128,512]{3,2,1,0:T(8,128)(2,1)}, u32[]{:S(2)}) copy-start(bf16[2,2,128,512]{3,2,1,0:T(8,128)(2,1)} %spec.1) | copy-start | bytes 1572868
  0.6 2.4 %copy-start.1 = (bf16[256,256]{1,0:T(8,128)(2,1)S(1)}, bf16[256,256]{1,0:T(8,128)(2,1)}, u32[]{:S(2)}) copy-start(bf16[256,256]{1,0:T(8,128)(2,1)} %constant.13.clone.inverse) | copy-start | bytes 393220
  0.7 2.4 %copy-start.2 = (bf16[256,256]{1,0:T(8,128)(2,1)S(1)}, bf16[256,256]{1,0:T(8,128)(2,1)}, u32[]{:S(2)}) copy-start(bf16[256,256]{1,0:T(8,128)(2,1)} %constant.12.clone.forward) | copy-start | bytes 393220
  0.7 2.4 %copy-start.3 = (f32[2,128,128]{2,1,0:T(8,128)S(1)}, f32[2,128,128]{2,1,0:T(8,128)}, u32[]{:S(2)}) copy-start(f32[2,128,128]{2,1,0:T(8,128)} %constant.11.clone.twid) | copy-start | bytes 393220
  0.7 2.4 %copy-start.4 = (bf16[512,64]{0,1:T(8,128)(2,1)S(1)}, bf16[512,64]{0,1:T(8,128)(2,1)}, u32[]{:S(2)}) copy-start(bf16[512,64]{0,1:T(8,128)(2,1)} %param.14) | copy-start | bytes 196612
  0.7 2.4 %copy-start.5 = (bf16[256,128]{1,0:T(8,128)(2,1)S(1)}, bf16[256,128]{1,0:T(8,128)(2,1)}, u32[]{:S(2)}) copy-start(bf16[256,128]{1,0:T(8,128)(2,1)} %constant.10.clone.first) | copy-start | bytes 196612
  0.7 2.4 %copy-start.6 = (bf16[64,256]{1,0:T(8,128)(2,1)S(1)}, bf16[64,256]{1,0:T(8,128)(2,1)}, u32[]{:S(2)}) copy-start(bf16[64,256]{1,0:T(8,128)(2,1)} %constant.14.clone.last) | copy-start | bytes 98308
  0.7 2.4 %copy-start.7 = (bf16[3,3,512]{2,1,0:T(4,128)(2,1)S(1)}, bf16[3,3,512]{2,1,0:T(4,128)(2,1)}, u32[]{:S(2)}) copy-start(bf16[3,3,512]{2,1,0:T(4,128)(2,1)} %taps.1) | copy-start | bytes 27652
  0.7 2.4 %copy-start.8 = (s32[128]{0:T(128)S(1)}, s32[128]{0:T(128)}, u32[]{:S(2)}) copy-start(s32[128]{0:T(128)} %param.10) | copy-start | bytes 1540

commit v3 on v2

--- a/solution.py
+++ b/solution.py
@@ -15,7 +15,8 @@
 SEQ = NX * NZ * NY
 TOK = 128
 CH = 512
-OWN = CH // SEQ
+GROUPS = SEQ // NZ
+OWN = CH // GROUPS
 LEN = 2 * SEQ * TOK
 NEAR_FIRST = (1, 7, 2, 6, 3, 5, 4)
 
@@ -42,9 +43,10 @@
 def kernel(
     ids, tab, taps, spec, wt, first, twid, forward, inverse, last,
     mixed, gated,
-    ids_in, spec_out, spec_in, spec_f, ext, sig_out, sig_in, conv_out, conv_in,
+    ids_in, spec_out, spec_in, spec_f, spec_c, ext, sig_out, sig_in, sig_f,
+    conv_f, conv_out, conv_in, query,
     gat, wy, wg, red_out, red_in,
-    s_ids, s_spec, s_sig, s_conv, s_wy, s_wyr, s_wx, s_wl, s_gat, s_red,
+    s_ids, s_spec, s_sig, s_query, s_conv, s_wy, s_wyr, s_wx, s_wl, s_gat, s_red,
 ):
     seq = lax.axis_index("seq")
     chan = lax.axis_index("chan")
@@ -55,11 +57,7 @@
         return px * (NZ * NY) + pz * NY + py
 
     def peer(k):
-        return seq_at(
-            lax.rem(x + k // (NZ * NY), NX),
-            lax.rem(zl + lax.rem(k // NY, NZ), NZ),
-            lax.rem(y + lax.rem(k, NY), NY),
-        )
+        return lax.rem(seq + k, SEQ)
 
     def remote(src, dst, sems, device):
         return pltpu.make_async_remote_copy(
@@ -93,9 +91,10 @@
             pieces = [
                 spec[r, a, :, cols].astype(F32).T.reshape(128 // OWN, OWN, 128) for a in range(2)
             ]
-            spec_out[pl.ds(j * (128 // OWN), 128 // OWN), pl.ds(r * 16, 16), :] = (
-                jnp.concatenate(pieces, 1).astype(BF16)
-            )
+            for a in range(2):
+                spec_out[pl.ds(j * (128 // OWN), 128 // OWN), pl.ds((2 * r + a) * OWN, OWN), :] = (
+                    pieces[a].astype(BF16)
+                )
 
     vocab = lax.broadcasted_iota(jnp.int32, (tab.shape[0], TOK), 0)
 
@@ -111,19 +110,33 @@
     ids_copy = remote(ids, ids_in, s_ids, {"seq": lax.rem(seq + 1, SEQ)})
     ids_copy.start()
 
-    def send_all(src, dst, sems):
+    active = zl == co
+    group = x * NY + y
+
+    def send_groups(src, dst, sems):
         def one(k, _):
-            d = peer(k)
-            remote(src.at[d], dst.at[seq], sems, {"seq": d}).start()
+            u = lax.rem(group + k, GROUPS)
+            to = {"seq": seq_at(u // NY, co, lax.rem(u, NY))}
+            remote(src.at[u], dst.at[seq], sems, to).start()
             return 0
 
-        lax.fori_loop(1, SEQ, one, 0)
-
-    def wait_all(src, dst, sems):
-        some = pl.ds(0, SEQ - 1)
-        copy = remote(src.at[some], dst.at[some], sems, other_z)
-        copy.wait_recv()
-        copy.wait_send()
+        lax.fori_loop(1, GROUPS, one, 0)
+
+        @pl.when(active)
+        def _():
+            dst[pl.ds(seq, 1)] = src[pl.ds(group, 1)]
+
+        @pl.when(jnp.logical_not(active))
+        def _():
+            remote(src.at[group], dst.at[seq], sems, other_z).start()
+
+    def wait_blocks(ref, count, sems, sent):
+        some = pl.ds(0, count)
+        copy = remote(ref.at[some], ref.at[some], sems, other_z)
+        if sent:
+            copy.wait_send()
+        else:
+            copy.wait_recv()
 
     ahead = 1 - 2 * co
     keeps = co == x // 2
@@ -165,8 +178,7 @@
     along_y(y, 1).start()
     along_y(y, -1).start()
     along_x(y)
-    send_all(spec_out, spec_in, s_spec)
-    spec_in[pl.ds(seq, 1)] = spec_out[pl.ds(seq, 1)]
+    send_groups(spec_out, spec_in, s_spec)
     weights_step(1)
 
     ids_copy.wait_recv()
@@ -183,51 +195,101 @@
         out = out + weights[1:2] * ext[g, pl.ds(7, TOK), :]
         return out + weights[2:3] * ext[g, pl.ds(6, TOK), :]
 
-    signal = (shortened(1) * shortened(2)).astype(BF16).astype(F32)
+    signal = shortened(1) * shortened(2)
     for j in range(CH // 128):
         block = signal[:, j * 128 : (j + 1) * 128].T
         n = 128 // OWN
-        sig_out[pl.ds(j * n, n)] = block.reshape(n, OWN, TOK)
-    send_all(sig_out, sig_in, s_sig)
-    sig_in[pl.ds(seq, 1)] = sig_out[pl.ds(seq, 1)]
+        sig_out[pl.ds(j * n, n)] = block.reshape(n, OWN, TOK).astype(BF16)
+    send_groups(sig_out, sig_in, s_sig)
+    query[pl.ds(zl, 1)] = shortened(0)[None]
+    query_copy = remote(query.at[zl], query.at[zl], s_query, other_z)
+    query_copy.start()
 
     weights_step(2)
     weights_step(3)
-    wait_all(spec_out, spec_in, s_spec)
-    spec_f[...] = spec_in[...].astype(F32)
+
+    @pl.when(active)
+    def _():
+        wait_blocks(spec_in, SEQ - 1, s_spec, False)
+        spec_f[...] = spec_in[...].astype(F32)
+        for c in range(OWN):
+            for n in range(4):
+                spec_c[c, n] = spec_f[:, OWN * n + c, :]
+
     weights_step(4)
-    wait_all(sig_out, sig_in, s_sig)
-    cos, sin = twid[0], twid[1]
-    for c in range(OWN):
-        s = sig_in[:, c, :].astype(BF16)
-        z = jnp.dot(first[...], jnp.concatenate([s, s], 0), preferred_element_type=F32)
-        zr, zi = z[:128], z[128:]
-        z = jnp.concatenate([zr * cos + zi * sin, zi * cos - zr * sin], 1).astype(BF16)
-        f = jnp.dot(z, forward[...], preferred_element_type=F32)
-        fr, fi = f[:, :128], f[:, 128:]
-        hr = jnp.concatenate([spec_f[:, c, :], spec_f[:, 8 + c, :]], 0)
-        hi = jnp.concatenate([spec_f[:, 16 + c, :], spec_f[:, 24 + c, :]], 0)
-        f = jnp.concatenate([fr * hr - fi * hi, fr * hi + fi * hr], 1).astype(BF16)
-        b = jnp.dot(f, inverse[...], preferred_element_type=F32)
-        br, bi = b[:, :128], b[:, 128:]
-        b = jnp.concatenate([br * cos - bi * sin, bi * cos + br * sin], 0).astype(BF16)
-        conv_out[:, c, :] = jnp.dot(last[...], b, preferred_element_type=F32)
-    send_all(conv_out, conv_in, s_conv)
-    conv_in[pl.ds(seq, 1)] = conv_out[pl.ds(seq, 1)]
-
-    query = shortened(0)
-    wait_all(conv_out, conv_in, s_conv)
-    for j in range(CH // 128):
-        n = 128 // OWN
-        block = conv_in[pl.ds(j * n, n)].reshape(128, TOK).T
-        value = (query[:, j * 128 : (j + 1) * 128] * block).astype(BF16)
-        gated[:, pl.ds(j * 128, 128)] = value
-        gat[pl.ds(zl, 1), pl.ds(co, 1), :, pl.ds(j * 128, 128)] = value[None, None]
-    own = gat.at[zl, co]
-    to_core = remote(own, own, s_gat.at[0], other_core)
-    to_core.start()
-    to_z = remote(own, own, s_gat.at[1], other_z)
-    to_z.start()
+
+    @pl.when(active)
+    def _():
+        wait_blocks(sig_in, SEQ - 1, s_sig, False)
+        sig_f[...] = sig_in[...].astype(F32)
+        cos, sin = twid[0], twid[1]
+        for start in range(0, OWN, 4):
+            some = range(start, start + 4)
+            lines = jnp.concatenate([sig_f[:, c, :] for c in some], 1).astype(BF16)
+            lines = jnp.concatenate([lines, lines], 0)
+            z_all = jnp.dot(first[...], lines, preferred_element_type=F32)
+            zs = []
+            for n in range(4):
+                zr, zi = z_all[:128, n * 128 : n * 128 + 128], z_all[128:, n * 128 : n * 128 + 128]
+                z = jnp.concatenate([zr * cos + zi * sin, zi * cos - zr * sin], 1)
+                zs.append(z.astype(BF16))
+            f_all = jnp.dot(jnp.concatenate(zs, 0), forward[...], preferred_element_type=F32)
+            fs = []
+            for n, c in enumerate(some):
+                fr, fi = f_all[n * 128 : n * 128 + 128, :128], f_all[n * 128 : n * 128 + 128, 128:]
+                hr = spec_c[c, :2].reshape(128, 128)
+                hi = spec_c[c, 2:].reshape(128, 128)
+                fs.append(jnp.concatenate([fr * hr - fi * hi, fr * hi + fi * hr], 1).astype(BF16))
+            b_all = jnp.dot(jnp.concatenate(fs, 0), inverse[...], preferred_element_type=F32)
+            bs = []
+            for n in range(4):
+                br, bi = b_all[n * 128 : n * 128 + 128, :128], b_all[n * 128 : n * 128 + 128, 128:]
+                b = jnp.concatenate([br * cos - bi * sin, bi * cos + br * sin], 0)
+                bs.append(b.astype(BF16))
+            out = jnp.dot(last[...], jnp.concatenate(bs, 1), preferred_element_type=F32)
+            for n, c in enumerate(some):
+                conv_f[:, c, :] = out[:, n * 128 : n * 128 + 128]
+        conv_out[...] = conv_f[...].astype(BF16)
+
+        def flip(d):
+            return d + NY * (1 - 2 * lax.rem(d // NY, NZ))
+
+        for turn in range(2):
+            def back(k, _):
+                d = lax.rem(seq + k, SEQ)
+                block = flip(d) if turn else d
+                remote(
+                    conv_out.at[block], conv_in.at[turn, group], s_conv.at[turn], {"seq": d}
+                ).start()
+                return 0
+
+            lax.fori_loop(1, SEQ, back, 0)
+            block = flip(seq) if turn else seq
+            conv_in[turn, pl.ds(group, 1)] = conv_out[pl.ds(block, 1)]
+
+    def gate(turn):
+        for count in (GROUPS - 1, GROUPS):
+            @pl.when(active == (count == GROUPS - 1))
+            def _():
+                wait_blocks(conv_in.at[turn], count, s_conv.at[turn], False)
+
+        t = 1 - zl if turn else zl
+        if turn:
+            query_copy.wait_recv()
+        for j in range(CH // 128):
+            n = 128 // OWN
+            cols = pl.ds(j * 128, 128)
+            block = conv_in[turn, pl.ds(j * n, n)].astype(F32).reshape(128, TOK).T
+            value = (query[t, :, cols] * block).astype(BF16)
+            if turn == 0:
+                gated[:, cols] = value
+            gat[turn, pl.ds(co, 1), :, cols] = value[None]
+        own = gat.at[turn, co]
+        to_core = remote(own, own, s_gat.at[turn], other_core)
+        to_core.start()
+        return to_core
+
+    to_cores = [gate(0)]
 
     for count in (3, 4):
         @pl.when(keeps == (count == 3))
@@ -239,20 +301,16 @@
     def _():
         pltpu.make_async_copy(wy, wg.at[2 * co + lax.rem(x, 2)], s_wl).wait()
 
-    to_core.wait_recv()
     for turn in range(2):
         t = zl if turn == 0 else 1 - zl
         if turn == 1:
-            to_z.wait_recv()
-            own = gat.at[1 - zl, co]
-            on = remote(own, own, s_gat.at[2], other_core)
-            on.start()
-            on.wait_recv()
+            to_cores.append(gate(1))
+        to_cores[turn].wait_recv()
         for i in range(2):
             total = jnp.zeros((TOK, CH), F32)
             for c in range(2):
                 total = total + lax.dot_general(
-                    gat[t, c], wg[2 * c + i].reshape(NY * 64, CH), (((1,), (1,)), ((), ())),
+                    gat[turn, c], wg[2 * c + i].reshape(NY * 64, CH), (((1,), (1,)), ((), ())),
                     preferred_element_type=F32,
                 )
             red_out[turn, i] = total.astype(BF16)
@@ -286,6 +344,17 @@
     mixed[...] = total.astype(BF16)
 
     ids_copy.wait_send()
+    for count in (GROUPS - 1, GROUPS):
+        @pl.when(active == (count == GROUPS - 1))
+        def _():
+            wait_blocks(spec_out, count, s_spec, True)
+            wait_blocks(sig_out, count, s_sig, True)
+
+    @pl.when(active)
+    def _():
+        for turn in range(2):
+            wait_blocks(conv_out, SEQ - 1, s_conv.at[turn], True)
+
     some = pl.ds(0, NY - 1)
     remote(wy.at[some], wy.at[some], s_wy, other_z).wait_send()
     for count in (3, 4):
@@ -294,9 +363,9 @@
             some = pl.ds(0, count)
             remote(wg.at[some], wg.at[some], s_wx, other_z).wait_send()
 
-    to_core.wait_send()
-    to_z.wait_send()
-    on.wait_send()
+    query_copy.wait_send()
+    for copy in to_cores:
+        copy.wait_send()
 
 
 def per_device(token_ids, vocab_table, short_taps, filter_spec, out_weight):
@@ -320,24 +389,30 @@
         out_specs=(vmem, vmem),
         scratch_shapes=[
             pltpu.VMEM((1, TOK), jnp.int32),
-            pltpu.VMEM((SEQ, 32, 128), BF16),
-            pltpu.VMEM((SEQ, 32, 128), BF16),
-            pltpu.VMEM((SEQ, 32, 128), F32),
+            pltpu.VMEM((GROUPS, 4 * OWN, 128), BF16),
+            pltpu.VMEM((SEQ, 4 * OWN, 128), BF16),
+            pltpu.VMEM((SEQ, 4 * OWN, 128), F32),
+            pltpu.VMEM((OWN, 4, SEQ, 128), F32),
             pltpu.VMEM((4, 8 + TOK, CH), F32),
+            pltpu.VMEM((GROUPS, OWN, TOK), BF16),
+            pltpu.VMEM((SEQ, OWN, TOK), BF16),
             pltpu.VMEM((SEQ, OWN, TOK), F32),
             pltpu.VMEM((SEQ, OWN, TOK), F32),
-            pltpu.VMEM((SEQ, OWN, TOK), F32),
-            pltpu.VMEM((SEQ, OWN, TOK), F32),
+            pltpu.VMEM((SEQ, OWN, TOK), BF16),
+            pltpu.VMEM((2, GROUPS, OWN, TOK), BF16),
+            pltpu.VMEM((NZ, TOK, CH), F32),
             pltpu.VMEM((NZ, 2, TOK, CH), BF16),
             pltpu.VMEM((NY, 64, CH), BF16),
             pltpu.VMEM((4, NY, 64, CH), BF16),
             pltpu.VMEM((2, 2, TOK, CH), BF16),
             pltpu.VMEM((NH, TOK, CH), BF16),
-            dma2, dma2, dma2, dma2, dma2,
+            dma2, dma2, dma2, dma2,
+            pltpu.SemaphoreType.DMA((2, 2)),
+            dma2,
             pltpu.SemaphoreType.DMA((NY,)),
             dma2,
             pltpu.SemaphoreType.DMA,
-            pltpu.SemaphoreType.DMA((3, 2)),
+            pltpu.SemaphoreType.DMA((2, 2)),
             dma2,
         ],
         compiler_params=pltpu.CompilerParams(

time: 74.6 us -> 70.5 us (0.945)
  Pallas kernels: 69.5 us -> 65.6 us
    pallas_call x1, Pallas kernels: 69.5 us -> 65.6 us  [per_device(): pl.pallas_call(kernel, out_shape=(out, out), in_specs=[vmem] * len(args),...]
where the time goes in v3:
time: 70.5 us; the launch traced here: 70.1 us
  Pallas kernels  65.6 us (93%)
  local copies, waits for them, and re-layouts  3.64 us (5%)
  between operations  0.79 us (1%)
    pallas_call x1, Pallas kernels, per_device(): pl.pallas_call(kernel, out_shape=(out, out), in_specs=[vmem] * len(args),...  65.6 us
    unnamed x21, local copies, waits for them, and re-layouts  3.64 us

profile of v3, /device:TPU:1, one launch (start us, length us, event | category | flops | bytes accessed | tf_op | source)
XLA Modules:
  0.0 70.1 jit_solution(17381287600099972270)
XLA Ops:
  0.6 0.0 copy-start
  0.6 0.0 copy-start.1
  0.7 0.0 copy-start.2
  0.7 0.0 copy-start.3
  0.7 0.0 copy-start.4
  0.7 0.0 copy-start.5
  0.7 0.0 copy-start.6
  0.7 0.0 copy-start.7
  0.7 0.0 copy-start.8
  0.7 2.3 %copy.12 = bf16[64,8,4,512]{3,1,2,0:T(8,128)(2,1)S(1)} copy(bf16[64,8,4,512]{3,2,1,0:T(4,128)(2,1)} %bitcast.7) | data formatting | bytes 4194304
  3.0 0.0 copy-done
  3.0 0.0 copy-done.1
  3.0 0.0 copy-done.2
  3.0 0.0 copy-done.3
  3.1 0.0 copy-done.4
  3.1 0.0 copy-done.5
  3.1 0.0 copy-done.6
  3.1 0.0 copy-done.7
  3.1 0.0 copy-done.8
  3.1 65.6 %hyena.1 = (bf16[128,512]{1,0:T(8,128)(2,1)S(1)}, bf16[128,512]{1,0:T(8,128)(2,1)S(1)}) custom-call(s32[1,128]{1,0:T(1,128)S(1)} %bitcast.6, bf16[512,2048]{1,0:T(8,128)(2,1)S(1)} %bitcast.4, bf16[3,3,512]{2,1,0:T(4,128)(2,1)S(1)} %copy-done.7, bf16[2,2,128,512]{3,2,1,0:T(8,128)(2,1)S(1)} %copy-done, bf16[64,512]{1,0:T(8,128)(2,1)S(1)} %bitcast.5, ...), custom_call_target="tpu_custom_call" | custom-call | tf_op jit(solution)/shard_map/hyena/pallas_call | solution.py:385
  68.7 0.7 copy.15
  69.4 0.7 copy.16
Async XLA Ops:
  0.6 2.4 %copy-start = (bf16[2,2,128,512]{3,2,1,0:T(8,128)(2,1)S(1)}, bf16[2,2,128,512]{3,2,1,0:T(8,128)(2,1)}, u32[]{:S(2)}) copy-start(bf16[2,2,128,512]{3,2,1,0:T(8,128)(2,1)} %spec.1) | copy-start | bytes 1572868
  0.6 2.4 %copy-start.1 = (bf16[256,256]{1,0:T(8,128)(2,1)S(1)}, bf16[256,256]{1,0:T(8,128)(2,1)}, u32[]{:S(2)}) copy-start(bf16[256,256]{1,0:T(8,128)(2,1)} %constant.13.clone.inverse) | copy-start | bytes 393220
  0.7 2.4 %copy-start.2 = (bf16[256,256]{1,0:T(8,128)(2,1)S(1)}, bf16[256,256]{1,0:T(8,128)(2,1)}, u32[]{:S(2)}) copy-start(bf16[256,256]{1,0:T(8,128)(2,1)} %constant.12.clone.forward) | copy-start | bytes 393220
  0.7 2.4 %copy-start.3 = (f32[2,128,128]{2,1,0:T(8,128)S(1)}, f32[2,128,128]{2,1,0:T(8,128)}, u32[]{:S(2)}) copy-start(f32[2,128,128]{2,1,0:T(8,128)} %constant.11.clone.twid) | copy-start | bytes 393220
  0.7 2.4 %copy-start.4 = (bf16[512,64]{0,1:T(8,128)(2,1)S(1)}, bf16[512,64]{0,1:T(8,128)(2,1)}, u32[]{:S(2)}) copy-start(bf16[512,64]{0,1:T(8,128)(2,1)} %param.14) | copy-start | bytes 196612
  0.7 2.4 %copy-start.5 = (bf16[256,128]{1,0:T(8,128)(2,1)S(1)}, bf16[256,128]{1,0:T(8,128)(2,1)}, u32[]{:S(2)}) copy-start(bf16[256,128]{1,0:T(8,128)(2,1)} %constant.10.clone.first) | copy-start | bytes 196612
  0.7 2.4 %copy-start.6 = (bf16[64,256]{1,0:T(8,128)(2,1)S(1)}, bf16[64,256]{1,0:T(8,128)(2,1)}, u32[]{:S(2)}) copy-start(bf16[64,256]{1,0:T(8,128)(2,1)} %constant.14.clone.last) | copy-start | bytes 98308
  0.7 2.4 %copy-start.7 = (bf16[3,3,512]{2,1,0:T(4,128)(2,1)S(1)}, bf16[3,3,512]{2,1,0:T(4,128)(2,1)}, u32[]{:S(2)}) copy-start(bf16[3,3,512]{2,1,0:T(4,128)(2,1)} %taps.1) | copy-start | bytes 27652
  0.7 2.4 %copy-start.8 = (s32[128]{0:T(128)S(1)}, s32[128]{0:T(128)}, u32[]{:S(2)}) copy-start(s32[128]{0:T(128)} %param.10) | copy-start | bytes 1540

commit v4 on v3

--- a/solution.py
+++ b/solution.py
@@ -40,6 +40,19 @@
     return first, twid, forward, inverse, last
 
 
+def each(start, stop, one, width=8):
+    steps = (stop - start) // width
+
+    def some(n, _):
+        for i in range(width):
+            one(start + n * width + i)
+        return 0
+
+    lax.fori_loop(0, steps, some, 0)
+    for k in range(start + steps * width, stop):
+        one(k)
+
+
 def kernel(
     ids, tab, taps, spec, wt, first, twid, forward, inverse, last,
     mixed, gated,
@@ -71,11 +84,10 @@
 
     barrier = pltpu.get_barrier_semaphore()
 
-    def greet(k, _):
+    def greet(k):
         pl.semaphore_signal(barrier, inc=1, device_id={"seq": peer(k)}, device_id_type=MESH)
-        return 0
-
-    lax.fori_loop(1, SEQ, greet, 0)
+
+    each(1, SEQ, greet)
     for k in range(NX):
         beside = {"seq": seq_at(lax.rem(x + k, NX), zl, y), "chan": zh * 2 + 1 - co}
         pl.semaphore_signal(barrier, inc=1, device_id=beside, device_id_type=MESH)
@@ -114,13 +126,12 @@
     group = x * NY + y
 
     def send_groups(src, dst, sems):
-        def one(k, _):
+        def one(k):
             u = lax.rem(group + k, GROUPS)
             to = {"seq": seq_at(u // NY, co, lax.rem(u, NY))}
             remote(src.at[u], dst.at[seq], sems, to).start()
-            return 0
-
-        lax.fori_loop(1, GROUPS, one, 0)
+
+        each(1, GROUPS, one)
 
         @pl.when(active)
         def _():
@@ -255,15 +266,14 @@
             return d + NY * (1 - 2 * lax.rem(d // NY, NZ))
 
         for turn in range(2):
-            def back(k, _):
+            def back(k):
                 d = lax.rem(seq + k, SEQ)
                 block = flip(d) if turn else d
                 remote(
                     conv_out.at[block], conv_in.at[turn, group], s_conv.at[turn], {"seq": d}
                 ).start()
-                return 0
-
-            lax.fori_loop(1, SEQ, back, 0)
+
+            each(1, SEQ, back)
             block = flip(seq) if turn else seq
             conv_in[turn, pl.ds(group, 1)] = conv_out[pl.ds(block, 1)]
 

time: 70.5 us -> 70.8 us (level)
  no operation moved by 1% of the time
where the time goes in v4:
time: 70.8 us; the launch traced here: 69.8 us
  Pallas kernels  65.4 us (92%)
  local copies, waits for them, and re-layouts  3.64 us (5%)
  between operations  0.79 us (1%)
    pallas_call x1, Pallas kernels, per_device(): pl.pallas_call(kernel, out_shape=(out, out), in_specs=[vmem] * len(args),...  65.4 us
    unnamed x21, local copies, waits for them, and re-layouts  3.64 us

profile of v4, /device:TPU:1, one launch (start us, length us, event | category | flops | bytes accessed | tf_op | source)
XLA Modules:
  0.0 69.8 jit_solution(9850270620811097527)
XLA Ops:
  0.6 0.0 copy-start
  0.6 0.0 copy-start.1
  0.7 0.0 copy-start.2
  0.7 0.0 copy-start.3
  0.7 0.0 copy-start.4
  0.7 0.0 copy-start.5
  0.7 0.0 copy-start.6
  0.7 0.0 copy-start.7
  0.7 0.0 copy-start.8
  0.7 2.3 %copy.12 = bf16[64,8,4,512]{3,1,2,0:T(8,128)(2,1)S(1)} copy(bf16[64,8,4,512]{3,2,1,0:T(4,128)(2,1)} %bitcast.7) | data formatting | bytes 4194304
  3.0 0.0 copy-done
  3.0 0.0 copy-done.1
  3.0 0.0 copy-done.2
  3.0 0.0 copy-done.3
  3.1 0.0 copy-done.4
  3.1 0.0 copy-done.5
  3.1 0.0 copy-done.6
  3.1 0.0 copy-done.7
  3.1 0.0 copy-done.8
  3.1 65.4 %hyena.1 = (bf16[128,512]{1,0:T(8,128)(2,1)S(1)}, bf16[128,512]{1,0:T(8,128)(2,1)S(1)}) custom-call(s32[1,128]{1,0:T(1,128)S(1)} %bitcast.6, bf16[512,2048]{1,0:T(8,128)(2,1)S(1)} %bitcast.4, bf16[3,3,512]{2,1,0:T(4,128)(2,1)S(1)} %copy-done.7, bf16[2,2,128,512]{3,2,1,0:T(8,128)(2,1)S(1)} %copy-done, bf16[64,512]{1,0:T(8,128)(2,1)S(1)} %bitcast.5, ...), custom_call_target="tpu_custom_call" | custom-call | tf_op jit(solution)/shard_map/hyena/pallas_call | solution.py:395
  68.5 0.7 copy.15
  69.2 0.7 copy.16
Async XLA Ops:
  0.6 2.4 %copy-start = (bf16[2,2,128,512]{3,2,1,0:T(8,128)(2,1)S(1)}, bf16[2,2,128,512]{3,2,1,0:T(8,128)(2,1)}, u32[]{:S(2)}) copy-start(bf16[2,2,128,512]{3,2,1,0:T(8,128)(2,1)} %spec.1) | copy-start | bytes 1572868
  0.6 2.4 %copy-start.1 = (bf16[256,256]{1,0:T(8,128)(2,1)S(1)}, bf16[256,256]{1,0:T(8,128)(2,1)}, u32[]{:S(2)}) copy-start(bf16[256,256]{1,0:T(8,128)(2,1)} %constant.13.clone.inverse) | copy-start | bytes 393220
  0.7 2.4 %copy-start.2 = (bf16[256,256]{1,0:T(8,128)(2,1)S(1)}, bf16[256,256]{1,0:T(8,128)(2,1)}, u32[]{:S(2)}) copy-start(bf16[256,256]{1,0:T(8,128)(2,1)} %constant.12.clone.forward) | copy-start | bytes 393220
  0.7 2.4 %copy-start.3 = (f32[2,128,128]{2,1,0:T(8,128)S(1)}, f32[2,128,128]{2,1,0:T(8,128)}, u32[]{:S(2)}) copy-start(f32[2,128,128]{2,1,0:T(8,128)} %constant.11.clone.twid) | copy-start | bytes 393220
  0.7 2.4 %copy-start.4 = (bf16[512,64]{0,1:T(8,128)(2,1)S(1)}, bf16[512,64]{0,1:T(8,128)(2,1)}, u32[]{:S(2)}) copy-start(bf16[512,64]{0,1:T(8,128)(2,1)} %param.14) | copy-start | bytes 196612
  0.7 2.4 %copy-start.5 = (bf16[256,128]{1,0:T(8,128)(2,1)S(1)}, bf16[256,128]{1,0:T(8,128)(2,1)}, u32[]{:S(2)}) copy-start(bf16[256,128]{1,0:T(8,128)(2,1)} %constant.10.clone.first) | copy-start | bytes 196612
  0.7 2.4 %copy-start.6 = (bf16[64,256]{1,0:T(8,128)(2,1)S(1)}, bf16[64,256]{1,0:T(8,128)(2,1)}, u32[]{:S(2)}) copy-start(bf16[64,256]{1,0:T(8,128)(2,1)} %constant.14.clone.last) | copy-start | bytes 98308
  0.7 2.4 %copy-start.7 = (bf16[3,3,512]{2,1,0:T(4,128)(2,1)S(1)}, bf16[3,3,512]{2,1,0:T(4,128)(2,1)}, u32[]{:S(2)}) copy-start(bf16[3,3,512]{2,1,0:T(4,128)(2,1)} %taps.1) | copy-start | bytes 27652
  0.7 2.4 %copy-start.8 = (s32[128]{0:T(128)S(1)}, s32[128]{0:T(128)}, u32[]{:S(2)}) copy-start(s32[128]{0:T(128)} %param.10) | copy-start | bytes 1540
